TPU v7x, 32 devices: a whole 2x2x4 slice. The times are simulated.
32 devices in a mesh: grp: 2 (over x), ctx: 16 (over z, y, core).
Axes of the slice: x: 2, y: 2, z: 4, core: 2. Of those that a mesh axis runs over, the one named last changes fastest.
Arguments:
- cotangent: bfloat16 [12288, 2048], P(('grp', 'ctx')), parts along dimension 0, may hold values from -6 to 6
- vis_count: int32 [32], P('grp'), parts along dimension 0, may hold values from 0 to 384, as said below
- vis_pos: int32 [12288], P(('grp', 'ctx')), parts along dimension 0, may hold values from 0 to 383, as said below
- patch_owner: int32 [6144], P('grp'), parts along dimension 0, may hold values from 0 to 15, as said below
- pre_act: bfloat16 [6144, 2304], P(('grp', 'ctx')), parts along dimension 0, may hold values from -6 to 6
- proj_weight: bfloat16 [2304, 2048], P('ctx'), may hold values from -0.125 to 0.125
Outputs:
- pre_act_grad: bfloat16 [6144, 2304], P(('grp', 'ctx')), parts along dimension 0
- hidden_bias_grad: float32 [4608], P('grp'), parts along dimension 0
- out_bias_grad: float32 [4096], P('grp'), parts along dimension 0
There are 2 independent parts, one for each index of `grp`. A program takes and returns all parts, laid end to end along the dimension named above; an argument that names none is the same for every part. Nothing has to cross between parts.
Inputs may be any that keep to these rules, and one draw needn't show every extreme that they name: `vis_count`: each entry is 16 times a whole number; the entries sum to 3072; the largest is 384. `vis_pos`: for each shard s the 384 entries from s * 384 are a permutation of the local positions: first the vis_count[s] visual positions in ascending order, then the others in ascending order. `patch_owner`: entry v is the context index of the device that holds visual token v; each aligned block of 16 entries names every index once, so every owner holds 192 visual tokens, token v in its row v // 16.
All inputs are finite; a program needn't handle non-finite values.
Results may differ from a plain program's by a relative error of at most 0.001.
Values may be sent and summed in bfloat16 or wider, within the bound.
A program may use at most 128 MiB of HBM per device.

v0:
```python
import math

import jax
import jax.numpy as jnp
from jax import lax
from jax.sharding import PartitionSpec as P


def gelu_tanh(values):
    return jax.nn.gelu(values, approximate=True)


def per_device(cotangent, vis_count, vis_pos, patch_owner, pre_act, proj_weight):
    ctx_size = lax.axis_size("ctx")
    my_index = lax.axis_index("ctx")
    tok_rows = cotangent.shape[0]
    row_width = cotangent.shape[1]
    per_peer = tok_rows // ctx_size
    owned_rows = pre_act.shape[0]
    loss_scale = 1.0 / math.sqrt(owned_rows * ctx_size)
    block_counts = vis_count // ctx_size
    first_block = jnp.cumsum(block_counts) - block_counts
    my_blocks = block_counts[my_index]
    my_first = first_block[my_index]
    ordered = jnp.take(cotangent, vis_pos, axis=0).reshape(per_peer, ctx_size, row_width)
    padded_owner = jnp.concatenate([patch_owner, jnp.zeros((tok_rows,), jnp.int32)]).reshape(
        -1, ctx_size
    )
    block_owner = lax.dynamic_slice_in_dim(padded_owner, my_first, per_peer, 0)
    live_blocks = jnp.arange(per_peer, dtype=jnp.int32) < my_blocks
    peer_ids = jnp.arange(ctx_size, dtype=jnp.int32)
    selector = (
        (block_owner[:, :, None] == peer_ids[None, None, :]) & live_blocks[:, None, None]
    ).astype(jnp.bfloat16)
    outgoing = jnp.einsum(
        "kro,krc->okc", selector, ordered, preferred_element_type=jnp.float32
    ).astype(jnp.bfloat16)
    incoming = lax.all_to_all(outgoing, "ctx", split_axis=0, concat_axis=0, tiled=True)
    received = incoming.reshape(ctx_size * per_peer, row_width)
    slot_ids = jnp.arange(owned_rows, dtype=jnp.int32)
    block_ends = first_block + block_counts
    slot_source = jnp.sum((block_ends[None, :] <= slot_ids[:, None]).astype(jnp.int32), axis=1)
    source_hits = slot_source[:, None] == peer_ids[None, :]
    slot_offset = jnp.sum(jnp.where(source_hits, first_block[None, :], 0), axis=1)
    flat_index = slot_source * per_peer + slot_ids - slot_offset
    buffer_ids = jnp.arange(ctx_size * per_peer, dtype=jnp.int32)
    buffer_source = buffer_ids // per_peer
    buffer_hits = buffer_source[:, None] == peer_ids[None, :]
    buffer_first = jnp.sum(jnp.where(buffer_hits, first_block[None, :], 0), axis=1)
    buffer_slot = jnp.minimum(buffer_first + buffer_ids % per_peer, owned_rows - 1)
    hidden_rows = jnp.take(pre_act, buffer_slot, axis=0)
    act_full, pullback = jax.vjp(gelu_tanh, hidden_rows.astype(jnp.float32))
    out_term = jnp.sum(received.astype(jnp.float32), axis=0) * loss_scale
    act_grad = lax.dot_general(
        received,
        lax.all_gather(proj_weight, "ctx", axis=0, tiled=True),
        (((1,), (1,)), ((), ())),
        preferred_element_type=jnp.float32,
    )
    hidden_grad = pullback(act_grad)[0]
    hidden_term = jnp.sum(hidden_grad, axis=0) * loss_scale
    rounded_grad = hidden_grad.astype(jnp.bfloat16)
    pre_act_grad = jnp.take(rounded_grad, flat_index, axis=0)
    hidden_bias_grad, out_bias_grad = lax.psum((hidden_term, out_term), "ctx")
    return (pre_act_grad, hidden_bias_grad, out_bias_grad)


def solution(mesh):
    return jax.shard_map(
        per_device,
        mesh=mesh,
        in_specs=(
            P(("grp", "ctx"), None),
            P("grp"),
            P(("grp", "ctx")),
            P("grp"),
            P(("grp", "ctx"), None),
            P("ctx", None),
        ),
        out_specs=(P(("grp", "ctx"), None), P("grp"), P("grp")),
        check_vma=False,
    )
```

profile of v0, /device:TPU:0, one launch (start us, length us, event | category | flops | bytes accessed | tf_op | source)
XLA Modules:
  0.0 199.3 jit_solution(8998298253554023529)
XLA Ops:
  7.2 0.7 all-gather.2.cloned.1.call-update
  7.9 0.7 fusion.33
  8.7 0.1 reduce.1
  8.8 0.7 fusion.32
  9.5 0.6 dynamic_slice.9
  11.4 0.7 concatenate.3
  12.1 0.1 reshape.152
  12.2 0.7 and_select_fusion.1
  12.9 0.6 dynamic_slice.11
  13.4 0.7 compare_and_fusion.1
  14.9 0.7 compare_select_fusion.3
  15.6 2.5 %gather_fusion = bf16[384,2048]{1,0:T(8,128)(2,1)S(1)} fusion(bf16[384,2048]{1,0:T(8,128)(2,1)S(1)} %copy-done, s32[1024]{0:T(1024)S(1)} %pad_clamp_fusion.2), kind=kCustom, calls=%fused_computation | custom fusion | bytes 3147264 | tf_op jit(solution)/shard_map/jit(_take)/gather | solution.py:25
  18.0 0.7 iota_compare_fusion.4
  18.7 0.6 fusion.8
  19.4 2.0 %copy.15 = bf16[16,24,2048]{2,1,0:T(8,128)(2,1)} copy(bf16[16,24,2048]{2,0,1:T(8,128)(2,1)S(1)} %fusion.8) | data formatting | bytes 3145728 | tf_op jit(solution)/shard_map/convert_element_type | solution.py:37
  21.4 7.4 %all-to-all-start = ((bf16[16,24,2048]{2,1,0:T(8,128)(2,1)}), bf16[16,24,2048]{2,1,0:T(8,128)(2,1)}, u32[]{:S(2)}, u32[]{:S(2)}) async-start(bf16[16,24,2048]{2,1,0:T(8,128)(2,1)} %copy.15), calls=%async_computation | async-start | bytes 3145728 | tf_op jit(solution)/shard_map/all_to_all | solution.py:38
  29.0 3.2 %gather_fusion.1 = bf16[384,2304]{1,0:T(8,128)(2,1)} fusion(bf16[192,2304]{1,0:T(8,128)(2,1)S(1)} %copy-done.1, s32[1024]{0:T(1024)S(1)} %pad_clamp_fusion.1), kind=kCustom, calls=%fused_computation.1 | custom fusion | bytes 3540480 | tf_op jit(solution)/shard_map/jit(_take)/gather | solution.py:51
  32.5 40.1 %all-to-all-done = bf16[16,24,2048]{2,1,0:T(8,128)(2,1)} async-done(((bf16[16,24,2048]{2,1,0:T(8,128)(2,1)}), bf16[16,24,2048]{2,1,0:T(8,128)(2,1)}, u32[]{:S(2)}, u32[]{:S(2)}) %all-to-all-start) | async-done | bytes 1572896 | tf_op jit(solution)/shard_map/all_to_all | solution.py:38
  72.6 1.7 convert_reduce_fusion
  74.3 43.6 %all-gather.2.cloned.1.call-done = bf16[2304,2048]{1,0:T(8,128)(2,1)} async-done(((bf16[144,2048]{1,0:T(8,128)(2,1)}), bf16[2304,2048]{1,0:T(8,128)(2,1)}) %all-gather.2.cloned.1.call-update) | async-done | bytes 9437200 | tf_op jit(solution)/shard_map/all_gather | solution.py:56
  117.9 10.5 %fusion.28 = (f32[2304]{0:T(1024)S(1)}, bf16[384,2304]{1,0:T(8,128)(2,1)S(1)}) fusion(bf16[384,2304]{1,0:T(8,128)(2,1)} %gather_fusion.1, pred[384]{0:T(512)(128)(4,1)S(1)} %compare_and_fusion, bf16[384,2048]{1,0:T(8,128)(2,1)} %bitcast.5, bf16[2304,2048]{1,0:T(8,128)(2,1)} %all-gather.2.cloned.1.call-done), kind=kOutput, calls=%fused_computation.69 | convolution fusion | flops 3644225280 | bytes 14558592 | tf_op jit(solution)/shard_map/dot_general | solution.py:54
  128.5 59.6 %all-reduce.1 = (f32[2304]{0:T(1024)}, f32[2048]{0:T(1024)}) all-reduce(f32[2304]{0:T(1024)S(1)} %broadcast_multiply_fusion, f32[2048]{0:T(1024)S(1)} %broadcast_multiply_fusion.1), channel_id=1, replica_groups=mesh['grp'=2,'ctx'=16] {'ctx'}, use_global_device_ids=true, to_apply=%region_5.6 | all-reduce | flops 4352 | bytes 34816 | tf_op jit(solution)/shard_map/psum | solution.py:64
  188.1 2.1 %gather_fusion.2 = bf16[192,2304]{1,0:T(8,128)(2,1)} fusion(bf16[384,2304]{1,0:T(8,128)(2,1)S(1)} %get-tuple-element.6, s32[1024]{0:T(1024)S(1)} %pad_clamp_fusion), kind=kCustom, calls=%fused_computation.2 | custom fusion | bytes 1770240 | tf_op jit(solution)/shard_map/jit(_take)/gather | solution.py:63
  190.2 2.2 %broadcast_select_fusion = bf16[192,2304]{1,0:T(8,128)(2,1)} fusion(bf16[192,2304]{1,0:T(8,128)(2,1)} %gather_fusion.2, pred[192]{0:T(512)(128)(4,1)S(1)} %compare_and_fusion.2), kind=kLoop, calls=%fused_computation.20 | loop fusion | flops 442368 | bytes 1769664 | tf_op jit(solution)/shard_map/jit(_take)/select_n | solution.py:63
  (23 shorter events, 0.7 us)
Async XLA Ops:
  7.2 8.4 %copy-start = (bf16[384,2048]{1,0:T(8,128)(2,1)S(1)}, bf16[384,2048]{1,0:T(8,128)(2,1)}, u32[]{:S(2)}) copy-start(bf16[384,2048]{1,0:T(8,128)(2,1)} %param.6) | copy-start | bytes 4718596
  7.2 110.7 %all-gather.2.cloned.1.call-start = ((), (), s32[]{:S(2)}) async-start(), calls=%async_computation.1 | async-start | bytes 10027008 | tf_op jit(solution)/shard_map/all_gather | solution.py:56
  19.3 9.6 %copy-start.1 = (bf16[192,2304]{1,0:T(8,128)(2,1)S(1)}, bf16[192,2304]{1,0:T(8,128)(2,1)}, u32[]{:S(2)}) copy-start(bf16[192,2304]{1,0:T(8,128)(2,1)} %param.10) | copy-start | bytes 2654212
  21.4 51.2 %all-to-all-start = ((bf16[16,24,2048]{2,1,0:T(8,128)(2,1)}), bf16[16,24,2048]{2,1,0:T(8,128)(2,1)}, u32[]{:S(2)}, u32[]{:S(2)}) async-start(bf16[16,24,2048]{2,1,0:T(8,128)(2,1)} %copy.15), calls=%async_computation | async-start | bytes 3145728 | tf_op jit(solution)/shard_map/all_to_all | solution.py:38
Sparse Core Ops, SparseCore 0:
  10.3 107.5 all-gather.1
where the time goes:
time: 200 us; the launch traced here: 199 us
  waiting for transfers between devices  84.5 us (42%)
  blocking collectives  59.6 us (30%)
  between operations  16.1 us (8%)
  local copies, waits for them, and re-layouts  12 us (6%)
  matrix products  11.1 us (6%)
  other arithmetic  8.44 us (4%)
  starting transfers between devices  7.47 us (4%)
    psum x1, blocking collectives, per_device(): hidden_bias_grad, out_bias_grad = lax.psum((hidden_term, out_term), 'ctx')  59.6 us
    all_gather x1, waiting for transfers between devices, per_device(): lax.all_gather(proj_weight, 'ctx', axis=0, tiled=True)  43.6 us
    all_to_all x1, waiting for transfers between devices, per_device(): lax.all_to_all(outgoing, 'ctx', split_axis=0, concat_axis=0, tiled=True)  40.1 us
    dot_general x1, matrix products, per_device(): lax.dot_general(received, lax.all_gather(proj_weight, 'ctx', axis=0, tile...  10.5 us
    all_to_all x1, starting transfers between devices, per_device(): lax.all_to_all(outgoing, 'ctx', split_axis=0, concat_axis=0, tiled=True)  7.43 us
  transfers between devices with their start and end apart: 2, of which 2 were waited for; matrix products, arithmetic and copies ran while one was open for 8% of the time, Pallas kernels for 0%

commit v1 on v0

v1 whole, which is shorter than its diff:
```python
import functools
import math

import jax
import jax.numpy as jnp
from jax import lax
from jax.experimental import pallas as pl
from jax.experimental.pallas import tpu as pltpu
from jax.sharding import PartitionSpec as P

QUARTERS = 4
MESH = pl.DeviceIdType.MESH


def gelu_slope(x):
    k = math.sqrt(2.0 / math.pi)
    square = x * x
    t = jnp.tanh(x * (k + (k * 0.044715) * square))
    return 0.5 * (1.0 + t) + (0.5 * x) * ((1.0 - t * t) * (k + (3.0 * 0.044715 * k) * square))


def kernel(
    grp_size,
    ctx_size,
    z_size,
    y_size,
    scale,
    target_ref,
    slot_ref,
    pos_ref,
    cot_ref,
    pre_ref,
    w_ref,
    out_ref,
    hidden_ref,
    bias_ref,
    w_all,
    outgoing,
    received,
    rows,
    bias_parts,
    hidden_parts,
    w_recv,
    z_send,
    y_send,
    x_send,
    s_send,
    row_send,
    row_recv,
    bias_send,
    bias_recv,
    hidden_send,
    hidden_recv,
):
    grp = lax.axis_index("grp")
    me = lax.axis_index("ctx")
    core = lax.rem(me, 2)
    chip = me // 2
    y = lax.rem(chip, y_size)
    z = chip // y_size
    chips = z_size * y_size
    shared = grp_size % 2 == 0
    own_quarters = QUARTERS // 2 if shared else QUARTERS
    half = lax.rem(grp, 2) if shared else 0
    first_quarter = half * own_quarters
    other_quarter = (1 - half) * own_quarters
    width = w_all.shape[3]
    tok_rows = cot_ref.shape[0]
    per_peer = tok_rows // ctx_size

    def index(z_at, y_at, core_at):
        return (z_at * y_size + y_at) * 2 + core_at

    sibling = {"ctx": index(z, y, 1 - core)}
    y_peer = {"ctx": index(z, y_size - 1 - y, core)}
    z_up = {"ctx": index(jnp.minimum(z + 1, z_size - 1), y, core)}
    z_down = {"ctx": index(jnp.maximum(z - 1, 0), y, core)}
    x_peer = {"grp": grp + 1 - 2 * lax.rem(grp, 2)}

    barrier = pltpu.get_barrier_semaphore()

    def greet(step, carry):
        pl.semaphore_signal(
            barrier, inc=1, device_id={"ctx": lax.rem(me + step, ctx_size)}, device_id_type=MESH
        )
        return carry

    lax.fori_loop(1, ctx_size, greet, 0)
    if shared:
        pl.semaphore_signal(barrier, inc=1, device_id=x_peer, device_id_type=MESH)
    for quarter in range(QUARTERS):
        w_all[quarter, me] = w_ref[:, quarter * width : (quarter + 1) * width]
    pl.semaphore_wait(barrier, ctx_size if shared else ctx_size - 1)

    def piece(quarter, origin, sem, device):
        return pltpu.make_async_remote_copy(
            src_ref=w_all.at[quarter, origin],
            dst_ref=w_all.at[quarter, origin],
            send_sem=sem,
            recv_sem=w_recv.at[quarter, origin],
            device_id=device,
            device_id_type=MESH,
        )

    def up(n, z_at):
        return piece(first_quarter + n, index(z_at, y, core), z_send.at[0, n, z_at], z_up)

    def down(n, z_at):
        return piece(first_quarter + n, index(z_at, y, core), z_send.at[1, n, z_at], z_down)

    def across(n, z_at):
        return piece(first_quarter + n, index(z_at, y, core), y_send.at[n, z_at], y_peer)

    def over(n, z_at, y_at):
        return piece(
            first_quarter + n,
            index(z_at, y_at, core),
            x_send.at[n, z_at * y_size + y_at],
            x_peer,
        )

    def beside(quarter, z_at, y_at):
        return piece(
            quarter, index(z_at, y_at, core), s_send.at[quarter, z_at * y_size + y_at], sibling
        )

    def arrived(quarter, origin):
        piece(quarter, origin, s_send.at[0, 0], sibling).wait_recv()

    for n in range(own_quarters):

        @pl.when(z < z_size - 1)
        def _():
            up(n, z).start()

        @pl.when(z > 0)
        def _():
            down(n, z).start()

        if y_size > 1:
            across(n, z).start()
    for quarter in range(QUARTERS):
        beside(quarter, z, y).start()

    slots = lax.broadcasted_iota(jnp.int32, (tok_rows, tok_rows), 0)
    to_slot = jnp.where(slots == target_ref[...], 1.0, 0.0).astype(jnp.bfloat16)
    to_pos = jnp.where(slots == pos_ref[...], 1.0, 0.0).astype(jnp.bfloat16)
    pick = lax.dot_general(
        to_slot, to_pos, (((1,), (1,)), ((), ())), preferred_element_type=jnp.float32
    ).astype(jnp.bfloat16)
    step_width = 512
    for at in range(0, cot_ref.shape[1], step_width):
        cols = slice(at, at + step_width)
        packed = jnp.dot(pick, cot_ref[:, cols], preferred_element_type=jnp.float32)
        outgoing[:, :, cols] = packed.astype(jnp.bfloat16).reshape(ctx_size, per_peer, step_width)
        bias_parts[me, :, cols] = jnp.sum(packed, axis=0, keepdims=True)

    def row_copy(step):
        peer = lax.rem(me + step, ctx_size)
        return pltpu.make_async_remote_copy(
            src_ref=outgoing.at[peer],
            dst_ref=received.at[me],
            send_sem=row_send.at[peer],
            recv_sem=row_recv.at[me],
            device_id={"ctx": peer},
            device_id_type=MESH,
        )

    def row_arrival(step):
        peer = lax.rem(me + step, ctx_size)
        return pltpu.make_async_remote_copy(
            src_ref=outgoing.at[peer],
            dst_ref=received.at[peer],
            send_sem=row_send.at[peer],
            recv_sem=row_recv.at[peer],
            device_id={"ctx": peer},
            device_id_type=MESH,
        )

    def part_copy(parts, send, recv, step, arrival):
        peer = lax.rem(me + step, ctx_size)
        slot = peer if arrival else me
        return pltpu.make_async_remote_copy(
            src_ref=parts.at[slot],
            dst_ref=parts.at[slot],
            send_sem=send.at[peer],
            recv_sem=recv.at[slot],
            device_id={"ctx": peer},
            device_id_type=MESH,
        )

    def each_peer(body):
        def run(step, carry):
            body(step)
            return carry

        lax.fori_loop(1, ctx_size, run, 0)

    def send_rows(step):
        row_copy(step).start()
        part_copy(bias_parts, bias_send, bias_recv, step, False).start()

    each_peer(send_rows)
    received[me] = outgoing[me]

    def pass_z(z_at, rising):
        for n in range(own_quarters):
            arrived(first_quarter + n, index(z_at, y, core))
            if rising:

                @pl.when(z < z_size - 1)
                def _():
                    up(n, z_at).start()

            else:

                @pl.when(z > 0)
                def _():
                    down(n, z_at).start()

            if y_size > 1:
                across(n, z_at).start()
            if shared:
                over(n, z_at, y).start()
            beside(first_quarter + n, z_at, y).start()

    def pass_y(z_at):
        for n in range(own_quarters):
            arrived(first_quarter + n, index(z_at, y_size - 1 - y, core))
            if shared:
                over(n, z_at, y_size - 1 - y).start()
            beside(first_quarter + n, z_at, y_size - 1 - y).start()

    def pass_x(z_at, y_at):
        for n in range(own_quarters):
            arrived(other_quarter + n, index(z_at, y_at, core))
            beside(other_quarter + n, z_at, y_at).start()

    def at_distance(d, body):
        @pl.when((d >= 0) & (z - d >= 0))
        def _():
            body(z - d, True)

        @pl.when((d > 0) & (z + d < z_size))
        def _():
            body(z + d, False)

    def forward(t, carry):
        @pl.when((t > 0) & (t < z_size))
        def _():
            at_distance(t, pass_z)

        if y_size > 1:

            @pl.when(t - 1 < z_size)
            def _():
                at_distance(t - 1, lambda z_at, rising: pass_y(z_at))

        if shared:

            def both(z_at, rising):
                @pl.when(z_at != z)
                def _():
                    pass_x(z_at, y)

                if y_size > 1:
                    pass_x(z_at, y_size - 1 - y)

            @pl.when(t - 2 < z_size)
            def _():
                at_distance(t - 2, both)

        return carry

    lax.fori_loop(1, z_size + 2, forward, 0)

    each_peer(lambda step: row_arrival(step).wait_recv())
    owned = rows.shape[0]
    slot_ids = lax.broadcasted_iota(jnp.int32, (owned, tok_rows), 0)
    place = jnp.where(slot_ids == slot_ref[...], 1.0, 0.0).astype(jnp.bfloat16)
    for at in range(0, cot_ref.shape[1], step_width):
        cols = slice(at, at + step_width)
        landed = received[:, :, cols].reshape(tok_rows, step_width)
        rows[:, cols] = jnp.dot(place, landed, preferred_element_type=jnp.float32).astype(
            jnp.bfloat16
        )

    def side(chip_at, carry):
        for quarter in range(QUARTERS):
            arrived(quarter, chip_at * 2 + 1 - core)
        return carry

    lax.fori_loop(0, chips, side, 0)

    group = ctx_size // 2
    units = group * w_all.shape[2]

    def multiply(at, carry):
        total = jnp.zeros((owned, units), jnp.float32)
        for quarter in range(QUARTERS):
            block = w_all[quarter, pl.ds(at * group, group)].reshape(units, width)
            total += lax.dot_general(
                rows[:, quarter * width : (quarter + 1) * width],
                block,
                (((1,), (1,)), ((), ())),
                preferred_element_type=jnp.float32,
            )
        cols = pl.ds(pl.multiple_of(at * units, 128), units)
        grad = total * gelu_slope(pre_ref[:, cols].astype(jnp.float32))
        out_ref[:, cols] = grad.astype(jnp.bfloat16)
        hidden_parts[me, :, cols] = jnp.sum(grad, axis=0, keepdims=True)
        return carry

    lax.fori_loop(0, 2, multiply, 0)
    each_peer(
        lambda step: part_copy(hidden_parts, hidden_send, hidden_recv, step, False).start()
    )

    each_peer(lambda step: part_copy(bias_parts, bias_send, bias_recv, step, True).wait_recv())
    bias_ref[...] = jnp.sum(bias_parts[...], axis=0) * scale

    def sent_z(z_at, carry):
        for n in range(own_quarters):

            @pl.when((z < z_size - 1) & (z_at <= z))
            def _():
                up(n, z_at).wait_send()

            @pl.when((z > 0) & (z_at >= z))
            def _():
                down(n, z_at).wait_send()

            if y_size > 1:
                across(n, z_at).wait_send()
        return carry

    lax.fori_loop(0, z_size, sent_z, 0)

    def sent_chip(chip_at, carry):
        z_at = chip_at // y_size
        y_at = lax.rem(chip_at, y_size)
        if shared:

            @pl.when(chip_at != chip)
            def _():
                for n in range(own_quarters):
                    over(n, z_at, y_at).wait_send()

        for quarter in range(QUARTERS):
            beside(quarter, z_at, y_at).wait_send()
        return carry

    lax.fori_loop(0, chips, sent_chip, 0)

    def sent_rows(step):
        row_copy(step).wait_send()
        part_copy(bias_parts, bias_send, bias_recv, step, False).wait_send()

    each_peer(sent_rows)
    each_peer(
        lambda step: part_copy(hidden_parts, hidden_send, hidden_recv, step, True).wait_recv()
    )
    hidden_ref[...] = jnp.sum(hidden_parts[...], axis=0) * scale
    each_peer(
        lambda step: part_copy(hidden_parts, hidden_send, hidden_recv, step, False).wait_send()
    )


def per_device(grp_size, cotangent, vis_count, vis_pos, patch_owner, pre_act, proj_weight):
    ctx_size = lax.axis_size("ctx")
    me = lax.axis_index("ctx")
    tok_rows, row_width = cotangent.shape
    per_peer = tok_rows // ctx_size
    owned, hidden = pre_act.shape
    units, _ = proj_weight.shape
    chips = ctx_size // 2
    y_size = 2 if chips == 8 else 1
    z_size = chips // y_size
    own_quarters = QUARTERS // 2 if grp_size % 2 == 0 else QUARTERS
    width = row_width // QUARTERS

    blocks = vis_count // ctx_size
    peers = jnp.arange(ctx_size, dtype=jnp.int32)
    first = jnp.sum(jnp.where(peers[None, :] < peers[:, None], blocks[None, :], 0), axis=1)
    my_first = jnp.sum(jnp.where(peers < me, blocks, 0))
    my_blocks = jnp.sum(jnp.where(peers == me, blocks, 0))
    padded = jnp.concatenate([patch_owner, jnp.zeros((tok_rows,), jnp.int32)])
    owner = lax.dynamic_slice_in_dim(padded, my_first * ctx_size, tok_rows, 0)
    block_at = jnp.arange(tok_rows, dtype=jnp.int32) // ctx_size
    target = jnp.where(block_at < my_blocks, owner * per_peer + block_at, -1)
    nth = jnp.arange(per_peer, dtype=jnp.int32)
    slot = jnp.where(nth[None, :] < blocks[:, None], first[:, None] + nth[None, :], -1)

    vmem = pl.BlockSpec(memory_space=pltpu.VMEM)
    dma = pltpu.SemaphoreType.DMA
    pre_act_grad, hidden_sum, out_sum = pl.pallas_call(
        functools.partial(
            kernel, grp_size, ctx_size, z_size, y_size, 1.0 / math.sqrt(owned * ctx_size)
        ),
        out_shape=(
            jax.ShapeDtypeStruct((owned, hidden), jnp.bfloat16),
            jax.ShapeDtypeStruct((1, hidden), jnp.float32),
            jax.ShapeDtypeStruct((1, row_width), jnp.float32),
        ),
        in_specs=[vmem] * 6,
        out_specs=(vmem, vmem, vmem),
        scratch_shapes=[
            pltpu.VMEM((QUARTERS, ctx_size, units, width), jnp.bfloat16),
            pltpu.VMEM((ctx_size, per_peer, row_width), jnp.bfloat16),
            pltpu.VMEM((ctx_size, per_peer, row_width), jnp.bfloat16),
            pltpu.VMEM((owned, row_width), jnp.bfloat16),
            pltpu.VMEM((ctx_size, 1, row_width), jnp.float32),
            pltpu.VMEM((ctx_size, 1, hidden), jnp.float32),
            dma((QUARTERS, ctx_size)),
            dma((2, own_quarters, z_size)),
            dma((own_quarters, z_size)),
            dma((own_quarters, chips)),
            dma((QUARTERS, chips)),
            dma((ctx_size,)),
            dma((ctx_size,)),
            dma((ctx_size,)),
            dma((ctx_size,)),
            dma((ctx_size,)),
            dma((ctx_size,)),
        ],
        compiler_params=pltpu.CompilerParams(
            collective_id=0, has_side_effects=True, vmem_limit_bytes=56 * 1024 * 1024
        ),
        cost_estimate=pl.CostEstimate(
            flops=2 * owned * hidden * row_width,
            bytes_accessed=8 * owned * row_width,
            transcendentals=owned * hidden,
        ),
    )(
        target.reshape(1, tok_rows),
        slot.reshape(1, tok_rows),
        vis_pos.reshape(1, tok_rows),
        cotangent,
        pre_act,
        proj_weight,
    )
    return (pre_act_grad, hidden_sum.reshape(hidden), out_sum.reshape(row_width))


def solution(mesh):
    return jax.shard_map(
        functools.partial(per_device, mesh.shape["grp"]),
        mesh=mesh,
        in_specs=(
            P(("grp", "ctx"), None),
            P("grp"),
            P(("grp", "ctx")),
            P("grp"),
            P(("grp", "ctx"), None),
            P("ctx", None),
        ),
        out_specs=(P(("grp", "ctx"), None), P("grp"), P("grp")),
        check_vma=False,
    )
```

time: 200 us -> 105 us (0.53)
  Pallas kernels: 0 us -> 93.8 us
  waiting for transfers between devices: 84.5 us -> 0 us
  blocking collectives: 59.6 us -> 0 us
  between operations: 16.1 us -> 1.31 us
  matrix products: 11.1 us -> 0 us
  starting transfers between devices: 7.47 us -> 0 us
  local copies, waits for them, and re-layouts: 12 us -> 5.2 us
  other arithmetic: 8.44 us -> 4.25 us
    pallas_call x0 -> x1, Pallas kernels: none -> 93.8 us  [per_device(): pl.pallas_call(functools.partial(kernel, grp_size, ctx_size, z_size, y_si...]
    psum x1 -> x0, blocking collectives: 59.6 us -> none  [per_device(): hidden_bias_grad, out_bias_grad = lax.psum((hidden_term, out_term), 'ctx')]
    all_gather x1 -> x0, waiting for transfers between devices: 43.6 us -> none  [per_device(): lax.all_gather(proj_weight, 'ctx', axis=0, tiled=True)]
    all_to_all x1 -> x0, waiting for transfers between devices: 40.1 us -> none  [per_device(): lax.all_to_all(outgoing, 'ctx', split_axis=0, concat_axis=0, tiled=True)]
    dot_general x2 -> x0, matrix products: 11.1 us -> none  [the longest x1 10.5 us: per_device(): lax.dot_general(received, lax.all_gather(proj_weight, 'ctx', axis=0, tile...]
    gather x3 -> x0, local copies, waits for them, and re-layouts: 7.8 us -> none  [the longest x1 3.24 us: per_device(): hidden_rows = jnp.take(pre_act, buffer_slot, axis=0)]
    all_to_all x1 -> x0, starting transfers between devices: 7.43 us -> none  [per_device(): lax.all_to_all(outgoing, 'ctx', split_axis=0, concat_axis=0, tiled=True)]
    unnamed x4, local copies, waits for them, and re-layouts: 0.02 us -> 2.74 us
  transfers between devices with their start and end apart: 2 -> 0, of which waited for: 2 -> 0; matrix products, arithmetic and copies ran while one was open for 8% -> 0% of each run, Pallas kernels for 0% -> 0%
where the time goes in v1:
time: 105 us
  Pallas kernels  93.8 us (89%)
  local copies, waits for them, and re-layouts  5.2 us (5%)
  other arithmetic  4.25 us (4%)
  between operations  1.31 us (1%)
    pallas_call x1, Pallas kernels, per_device(): pl.pallas_call(functools.partial(kernel, grp_size, ctx_size, z_size, y_si...  93.8 us
    unnamed x4, local copies, waits for them, and re-layouts  2.74 us

profile of v1, /device:TPU:0, one launch (start us, length us, event | category | flops | bytes accessed | tf_op | source)
XLA Modules:
  0.0 104.6 jit_solution(1442654932694775303)
XLA Ops:
  0.6 1.3 %fusion.7 = (s32[]{:T(128)}, s32[]{:T(128)}, s32[16]{0:T(128)S(1)}) fusion(s32[]{:T(128)S(6)} %axis_index.12, s32[16]{0:T(128)} %param.7), kind=kLoop, calls=%fused_computation.22 | loop fusion | flops 334 | bytes 140 | tf_op jit(solution)/shard_map/reduce_sum | solution.py:386
  2.6 0.1 select_reduce_fusion
  2.7 1.4 %fusion.4 = s32[384]{0:T(512)S(1)} fusion(s32[]{:T(128)S(6)} %select_n.48, s32[3072]{0:T(1024)} %param.9, s32[]{:T(128)} %get-tuple-element.9), kind=kLoop, calls=%fused_computation.13 | loop fusion | flops 4608 | bytes 13832 | tf_op jit(solution)/shard_map/jit(_where)/select_n | solution.py:390
  4.1 0.6 reshape.71.target_ref
  4.7 1.2 %reshape.72.pos_ref = s32[1,384]{1,0:T(1,128)} reshape(s32[384]{0:T(512)} %param.8) | data formatting | bytes 3072 | tf_op jit(solution)/shard_map/reshape | solution.py:437
  5.9 0.1 add_select_fusion
  6.0 0.7 select_n.52.slot_ref
  6.7 93.8 %shard_map.85 = (bf16[192,2304]{1,0:T(8,128)(2,1)}, f32[1,2304]{1,0:T(1,128)}, f32[1,2048]{1,0:T(1,128)}) custom-call(s32[1,384]{1,0:T(1,128)} %reshape.71.target_ref, s32[1,384]{1,0:T(1,128)} %select_n.52.slot_ref, s32[1,384]{1,0:T(1,128)} %reshape.72.pos_ref, bf16[384,2048]{1,0:T(8,128)(2,1)} %cot_ref.1, bf16[192,2304]{1,0:T(8,128)(2,1)} %pre_ref.1, ...), custom_call_target="tpu_custom_call" | custom-call | flops 1811939328 | bytes 3145728 | tf_op jit(solution)/shard_map/pallas_call | solution.py:396
  100.5 0.0 copy-start
  100.5 1.3 %reduce = f32[2304]{0:T(1024)} reduce(f32[1,2304]{1,0:T(1,128)} %get-tuple-element.7, f32[]{:T(128)} %constant.41), dimensions={0}, to_apply=%get-tuple-element.7.reduce_sub_computation | reduce | bytes 18436 | tf_op jit(solution)/shard_map/pallas_call | solution.py:396
  101.8 2.1 %copy.11 = bf16[192,2304]{1,0:T(8,128)(2,1)} copy(bf16[192,2304]{1,0:T(8,128)(2,1)} %get-tuple-element.15) | data formatting | bytes 1769472
  104.0 0.0 copy-done
  104.0 0.6 copy.12
Async XLA Ops:
  100.5 3.5 %copy-start = (f32[1,2048]{1,0:T(1,128)S(1)}, f32[1,2048]{1,0:T(1,128)}, u32[]{:S(2)}) copy-start(f32[1,2048]{1,0:T(1,128)} %get-tuple-element.8) | copy-start | bytes 24580

commit v2 on v1

--- a/solution.py
+++ b/solution.py
@@ -8,7 +8,9 @@
 from jax.experimental.pallas import tpu as pltpu
 from jax.sharding import PartitionSpec as P
 
-QUARTERS = 4
+PIECES = 8
+SWAPPED = 4
+ROW_FROM = 1
 MESH = pl.DeviceIdType.MESH
 
 
@@ -25,21 +27,24 @@
     z_size,
     y_size,
     scale,
-    target_ref,
-    slot_ref,
+    count_ref,
     pos_ref,
-    cot_ref,
-    pre_ref,
-    w_ref,
+    owner_ref,
+    cot_hbm,
+    pre_hbm,
+    w_hbm,
     out_ref,
     hidden_ref,
     bias_ref,
+    cot_ref,
+    pre_ref,
     w_all,
     outgoing,
     received,
     rows,
     bias_parts,
     hidden_parts,
+    load_sem,
     w_recv,
     z_send,
     y_send,
@@ -60,13 +65,18 @@
     z = chip // y_size
     chips = z_size * y_size
     shared = grp_size % 2 == 0
-    own_quarters = QUARTERS // 2 if shared else QUARTERS
+    swapped = SWAPPED if shared else 0
+    own_pieces = PIECES - swapped
     half = lax.rem(grp, 2) if shared else 0
-    first_quarter = half * own_quarters
-    other_quarter = (1 - half) * own_quarters
     width = w_all.shape[3]
     tok_rows = cot_ref.shape[0]
     per_peer = tok_rows // ctx_size
+
+    def own_piece(n):
+        return half * swapped + n if n < swapped else swapped + n
+
+    def other_piece(n):
+        return (1 - half) * swapped + n
 
     def index(z_at, y_at, core_at):
         return (z_at * y_size + y_at) * 2 + core_at
@@ -77,6 +87,14 @@
     z_down = {"ctx": index(jnp.maximum(z - 1, 0), y, core)}
     x_peer = {"grp": grp + 1 - 2 * lax.rem(grp, 2)}
 
+    own_shard = [
+        pltpu.make_async_copy(
+            w_hbm.at[:, pl.ds(at * width, width)], w_all.at[at, me], load_sem.at[at]
+        )
+        for at in range(PIECES)
+    ]
+    for load in own_shard:
+        load.start()
     barrier = pltpu.get_barrier_semaphore()
 
     def greet(step, carry):
@@ -88,8 +106,12 @@
     lax.fori_loop(1, ctx_size, greet, 0)
     if shared:
         pl.semaphore_signal(barrier, inc=1, device_id=x_peer, device_id_type=MESH)
-    for quarter in range(QUARTERS):
-        w_all[quarter, me] = w_ref[:, quarter * width : (quarter + 1) * width]
+    loads = [pltpu.make_async_copy(cot_hbm, cot_ref, load_sem.at[PIECES])]
+    loads += [pltpu.make_async_copy(pre_hbm, pre_ref, load_sem.at[PIECES + 1])]
+    for load in loads:
+        load.start()
+    for load in own_shard:
+        load.wait()
     pl.semaphore_wait(barrier, ctx_size if shared else ctx_size - 1)
 
     def piece(quarter, origin, sem, device):
@@ -103,17 +125,17 @@
         )
 
     def up(n, z_at):
-        return piece(first_quarter + n, index(z_at, y, core), z_send.at[0, n, z_at], z_up)
+        return piece(own_piece(n), index(z_at, y, core), z_send.at[0, n, z_at], z_up)
 
     def down(n, z_at):
-        return piece(first_quarter + n, index(z_at, y, core), z_send.at[1, n, z_at], z_down)
+        return piece(own_piece(n), index(z_at, y, core), z_send.at[1, n, z_at], z_down)
 
     def across(n, z_at):
-        return piece(first_quarter + n, index(z_at, y, core), y_send.at[n, z_at], y_peer)
+        return piece(own_piece(n), index(z_at, y, core), y_send.at[n, z_at], y_peer)
 
     def over(n, z_at, y_at):
         return piece(
-            first_quarter + n,
+            own_piece(n),
             index(z_at, y_at, core),
             x_send.at[n, z_at * y_size + y_at],
             x_peer,
@@ -127,7 +149,7 @@
     def arrived(quarter, origin):
         piece(quarter, origin, s_send.at[0, 0], sibling).wait_recv()
 
-    for n in range(own_quarters):
+    for n in range(own_pieces):
 
         @pl.when(z < z_size - 1)
         def _():
@@ -139,12 +161,47 @@
 
         if y_size > 1:
             across(n, z).start()
-    for quarter in range(QUARTERS):
+    for quarter in range(PIECES):
         beside(quarter, z, y).start()
 
+    blocks = lax.div(count_ref[...].reshape(1, ctx_size), ctx_size).astype(jnp.float32)
+    peers = lax.broadcasted_iota(jnp.int32, (1, ctx_size), 1)
+    my_first = jnp.sum(jnp.where(peers < me, blocks, 0.0), axis=1, keepdims=True)
+    my_blocks = jnp.sum(jnp.where(peers == me, blocks, 0.0), axis=1, keepdims=True)
+    token = lax.broadcasted_iota(jnp.int32, (1, tok_rows), 1)
+    start = (my_first * ctx_size).astype(jnp.int32)
+    chunk = math.gcd(owner_ref.shape[0], 1024)
+    offset = lax.broadcasted_iota(jnp.int32, (chunk, tok_rows), 0) - lax.broadcasted_iota(
+        jnp.int32, (chunk, tok_rows), 1
+    )
+    owner = jnp.zeros((8, tok_rows), jnp.float32)
+    for at in range(0, owner_ref.shape[0], chunk):
+        part = owner_ref[at : at + chunk].reshape(1, chunk).astype(jnp.float32)
+        part = jnp.broadcast_to(part, (8, chunk)).astype(jnp.bfloat16)
+        hit = jnp.where(offset == start - at, 1.0, 0.0).astype(jnp.bfloat16)
+        owner += jnp.dot(part, hit, preferred_element_type=jnp.float32)
+    nth_block = lax.div(token, ctx_size)
+    target = jnp.where(
+        nth_block.astype(jnp.float32) < my_blocks,
+        owner[0:1].astype(jnp.int32) * per_peer + nth_block,
+        -1,
+    )
+
+    source = lax.div(token, per_peer)
+    nth = (token - source * per_peer).astype(jnp.float32)
+    peer_rows = lax.broadcasted_iota(jnp.int32, (ctx_size, tok_rows), 0)
+    counts = jnp.broadcast_to(blocks, (8, ctx_size)).astype(jnp.bfloat16)
+    before = jnp.where(peer_rows < source, 1.0, 0.0).astype(jnp.bfloat16)
+    equal = jnp.where(peer_rows == source, 1.0, 0.0).astype(jnp.bfloat16)
+    first = jnp.dot(counts, before, preferred_element_type=jnp.float32)[0:1]
+    held = jnp.dot(counts, equal, preferred_element_type=jnp.float32)[0:1]
+    slot = jnp.where(nth < held, first + nth, -1.0).astype(jnp.int32)
+
+    for load in loads:
+        load.wait()
     slots = lax.broadcasted_iota(jnp.int32, (tok_rows, tok_rows), 0)
-    to_slot = jnp.where(slots == target_ref[...], 1.0, 0.0).astype(jnp.bfloat16)
-    to_pos = jnp.where(slots == pos_ref[...], 1.0, 0.0).astype(jnp.bfloat16)
+    to_slot = jnp.where(slots == target, 1.0, 0.0).astype(jnp.bfloat16)
+    to_pos = jnp.where(slots == pos_ref[...].reshape(1, tok_rows), 1.0, 0.0).astype(jnp.bfloat16)
     pick = lax.dot_general(
         to_slot, to_pos, (((1,), (1,)), ((), ())), preferred_element_type=jnp.float32
     ).astype(jnp.bfloat16)
@@ -200,12 +257,26 @@
         row_copy(step).start()
         part_copy(bias_parts, bias_send, bias_recv, step, False).start()
 
-    each_peer(send_rows)
     received[me] = outgoing[me]
+    batch = -(-(ctx_size - 1) // (z_size + 2 - ROW_FROM))
+
+    def send_batch(t):
+        @pl.when(t >= ROW_FROM)
+        def _():
+            def run(at, carry):
+                step = (t - ROW_FROM) * batch + at + 1
+
+                @pl.when(step < ctx_size)
+                def _():
+                    send_rows(step)
+
+                return carry
+
+            lax.fori_loop(0, batch, run, 0)
 
     def pass_z(z_at, rising):
-        for n in range(own_quarters):
-            arrived(first_quarter + n, index(z_at, y, core))
+        for n in range(own_pieces):
+            arrived(own_piece(n), index(z_at, y, core))
             if rising:
 
                 @pl.when(z < z_size - 1)
@@ -220,21 +291,21 @@
 
             if y_size > 1:
                 across(n, z_at).start()
-            if shared:
+            if n < swapped:
                 over(n, z_at, y).start()
-            beside(first_quarter + n, z_at, y).start()
+            beside(own_piece(n), z_at, y).start()
 
     def pass_y(z_at):
-        for n in range(own_quarters):
-            arrived(first_quarter + n, index(z_at, y_size - 1 - y, core))
-            if shared:
+        for n in range(own_pieces):
+            arrived(own_piece(n), index(z_at, y_size - 1 - y, core))
+            if n < swapped:
                 over(n, z_at, y_size - 1 - y).start()
-            beside(first_quarter + n, z_at, y_size - 1 - y).start()
+            beside(own_piece(n), z_at, y_size - 1 - y).start()
 
     def pass_x(z_at, y_at):
-        for n in range(own_quarters):
-            arrived(other_quarter + n, index(z_at, y_at, core))
-            beside(other_quarter + n, z_at, y_at).start()
+        for n in range(swapped):
+            arrived(other_piece(n), index(z_at, y_at, core))
+            beside(other_piece(n), z_at, y_at).start()
 
     def at_distance(d, body):
         @pl.when((d >= 0) & (z - d >= 0))
@@ -246,6 +317,7 @@
             body(z + d, False)
 
     def forward(t, carry):
+        send_batch(t)
         @pl.when((t > 0) & (t < z_size))
         def _():
             at_distance(t, pass_z)
@@ -277,7 +349,7 @@
     each_peer(lambda step: row_arrival(step).wait_recv())
     owned = rows.shape[0]
     slot_ids = lax.broadcasted_iota(jnp.int32, (owned, tok_rows), 0)
-    place = jnp.where(slot_ids == slot_ref[...], 1.0, 0.0).astype(jnp.bfloat16)
+    place = jnp.where(slot_ids == slot, 1.0, 0.0).astype(jnp.bfloat16)
     for at in range(0, cot_ref.shape[1], step_width):
         cols = slice(at, at + step_width)
         landed = received[:, :, cols].reshape(tok_rows, step_width)
@@ -286,7 +358,7 @@
         )
 
     def side(chip_at, carry):
-        for quarter in range(QUARTERS):
+        for quarter in range(PIECES):
             arrived(quarter, chip_at * 2 + 1 - core)
         return carry
 
@@ -297,7 +369,7 @@
 
     def multiply(at, carry):
         total = jnp.zeros((owned, units), jnp.float32)
-        for quarter in range(QUARTERS):
+        for quarter in range(PIECES):
             block = w_all[quarter, pl.ds(at * group, group)].reshape(units, width)
             total += lax.dot_general(
                 rows[:, quarter * width : (quarter + 1) * width],
@@ -320,7 +392,7 @@
     bias_ref[...] = jnp.sum(bias_parts[...], axis=0) * scale
 
     def sent_z(z_at, carry):
-        for n in range(own_quarters):
+        for n in range(own_pieces):
 
             @pl.when((z < z_size - 1) & (z_at <= z))
             def _():
@@ -343,10 +415,10 @@
 
             @pl.when(chip_at != chip)
             def _():
-                for n in range(own_quarters):
+                for n in range(swapped):
                     over(n, z_at, y_at).wait_send()
 
-        for quarter in range(QUARTERS):
+        for quarter in range(PIECES):
             beside(quarter, z_at, y_at).wait_send()
         return carry
 
@@ -368,7 +440,6 @@
 
 def per_device(grp_size, cotangent, vis_count, vis_pos, patch_owner, pre_act, proj_weight):
     ctx_size = lax.axis_size("ctx")
-    me = lax.axis_index("ctx")
     tok_rows, row_width = cotangent.shape
     per_peer = tok_rows // ctx_size
     owned, hidden = pre_act.shape
@@ -376,20 +447,9 @@
     chips = ctx_size // 2
     y_size = 2 if chips == 8 else 1
     z_size = chips // y_size
-    own_quarters = QUARTERS // 2 if grp_size % 2 == 0 else QUARTERS
-    width = row_width // QUARTERS
-
-    blocks = vis_count // ctx_size
-    peers = jnp.arange(ctx_size, dtype=jnp.int32)
-    first = jnp.sum(jnp.where(peers[None, :] < peers[:, None], blocks[None, :], 0), axis=1)
-    my_first = jnp.sum(jnp.where(peers < me, blocks, 0))
-    my_blocks = jnp.sum(jnp.where(peers == me, blocks, 0))
-    padded = jnp.concatenate([patch_owner, jnp.zeros((tok_rows,), jnp.int32)])
-    owner = lax.dynamic_slice_in_dim(padded, my_first * ctx_size, tok_rows, 0)
-    block_at = jnp.arange(tok_rows, dtype=jnp.int32) // ctx_size
-    target = jnp.where(block_at < my_blocks, owner * per_peer + block_at, -1)
-    nth = jnp.arange(per_peer, dtype=jnp.int32)
-    slot = jnp.where(nth[None, :] < blocks[:, None], first[:, None] + nth[None, :], -1)
+    swapped = SWAPPED if grp_size % 2 == 0 else 0
+    own_pieces = PIECES - swapped
+    width = row_width // PIECES
 
     vmem = pl.BlockSpec(memory_space=pltpu.VMEM)
     dma = pltpu.SemaphoreType.DMA
@@ -402,20 +462,23 @@
             jax.ShapeDtypeStruct((1, hidden), jnp.float32),
             jax.ShapeDtypeStruct((1, row_width), jnp.float32),
         ),
-        in_specs=[vmem] * 6,
+        in_specs=[vmem] * 3 + [pl.BlockSpec(memory_space=pl.ANY)] * 3,
         out_specs=(vmem, vmem, vmem),
         scratch_shapes=[
-            pltpu.VMEM((QUARTERS, ctx_size, units, width), jnp.bfloat16),
+            pltpu.VMEM((tok_rows, row_width), jnp.bfloat16),
+            pltpu.VMEM((owned, hidden), jnp.bfloat16),
+            pltpu.VMEM((PIECES, ctx_size, units, width), jnp.bfloat16),
             pltpu.VMEM((ctx_size, per_peer, row_width), jnp.bfloat16),
             pltpu.VMEM((ctx_size, per_peer, row_width), jnp.bfloat16),
             pltpu.VMEM((owned, row_width), jnp.bfloat16),
             pltpu.VMEM((ctx_size, 1, row_width), jnp.float32),
             pltpu.VMEM((ctx_size, 1, hidden), jnp.float32),
-            dma((QUARTERS, ctx_size)),
-            dma((2, own_quarters, z_size)),
-            dma((own_quarters, z_size)),
-            dma((own_quarters, chips)),
-            dma((QUARTERS, chips)),
+            dma((PIECES + 2,)),
+            dma((PIECES, ctx_size)),
+            dma((2, own_pieces, z_size)),
+            dma((own_pieces, z_size)),
+            dma((max(swapped, 1), chips)),
+            dma((PIECES, chips)),
             dma((ctx_size,)),
             dma((ctx_size,)),
             dma((ctx_size,)),
@@ -432,9 +495,9 @@
             transcendentals=owned * hidden,
         ),
     )(
-        target.reshape(1, tok_rows),
-        slot.reshape(1, tok_rows),
-        vis_pos.reshape(1, tok_rows),
+        vis_count,
+        vis_pos,
+        patch_owner,
         cotangent,
         pre_act,
         proj_weight,

time: 105 us -> 85 us (0.81)
  Pallas kernels: 93.8 us -> 80 us
  other arithmetic: 4.25 us -> 1.33 us
  local copies, waits for them, and re-layouts: 5.2 us -> 2.74 us
    pallas_call x1, Pallas kernels: 93.8 us -> 80 us  [per_device(): pl.pallas_call(functools.partial(kernel, grp_size, ctx_size, z_size, y_si...]
    reshape x2 -> x0, local copies, waits for them, and re-layouts: 1.81 us -> none  [the longest x1 1.24 us: per_device(): vis_pos.reshape(1, tok_rows)]
    select_n x2 -> x0, other arithmetic: 1.5 us -> none  [the longest x1 1.43 us: per_device(): target = jnp.where(block_at < my_blocks, owner * per_peer + block_at, -1)]
    reduce_sum x2 -> x0, other arithmetic: 1.42 us -> none  [the longest x1 1.3 us: per_device(): my_blocks = jnp.sum(jnp.where(peers == me, blocks, 0))]
where the time goes in v2:
time: 85 us; the launch traced here: 84.7 us
  Pallas kernels  80 us (94%)
  local copies, waits for them, and re-layouts  2.74 us (3%)
  other arithmetic  1.33 us (2%)
    pallas_call x1, Pallas kernels, per_device(): pl.pallas_call(functools.partial(kernel, grp_size, ctx_size, z_size, y_si...  80 us
    unnamed x4, local copies, waits for them, and re-layouts  2.74 us

profile of v2, /device:TPU:0, one launch (start us, length us, event | category | flops | bytes accessed | tf_op | source)
XLA Modules:
  0.0 84.7 jit_solution(14829865200938502205)
XLA Ops:
  0.6 80.0 %shard_map.85 = (bf16[192,2304]{1,0:T(8,128)(2,1)}, f32[1,2304]{1,0:T(1,128)}, f32[1,2048]{1,0:T(1,128)}) custom-call(s32[16]{0:T(128)} %count_ref.1, s32[384]{0:T(512)} %pos_ref.1, s32[3072]{0:T(1024)} %owner_ref.1, bf16[384,2048]{1,0:T(8,128)(2,1)} %cot_hbm.1, bf16[192,2304]{1,0:T(8,128)(2,1)} %pre_hbm.1, bf16[144,2048]{1,0:T(8,128)(2,1)} %w_hbm.1), custom_call_target="tpu_custom_call" | custom-call | flops 1811939328 | bytes 3145728 | tf_op jit(solution)/shard_map/pallas_call | solution.py:456
  80.6 0.0 copy-start
  80.6 1.3 %reduce = f32[2304]{0:T(1024)} reduce(f32[1,2304]{1,0:T(1,128)} %get-tuple-element.7, f32[]{:T(128)} %constant), dimensions={0}, to_apply=%get-tuple-element.7.reduce_sub_computation | reduce | bytes 18436 | tf_op jit(solution)/shard_map/pallas_call | solution.py:456
  82.0 2.1 %copy.11 = bf16[192,2304]{1,0:T(8,128)(2,1)} copy(bf16[192,2304]{1,0:T(8,128)(2,1)} %get-tuple-element.12) | data formatting | bytes 1769472
  84.1 0.0 copy-done
  84.1 0.6 copy.12
Async XLA Ops:
  80.6 3.5 %copy-start = (f32[1,2048]{1,0:T(1,128)S(1)}, f32[1,2048]{1,0:T(1,128)}, u32[]{:S(2)}) copy-start(f32[1,2048]{1,0:T(1,128)} %get-tuple-element.8) | copy-start | bytes 24580

commit v3 on v2

--- a/solution.py
+++ b/solution.py
@@ -258,54 +258,47 @@
         part_copy(bias_parts, bias_send, bias_recv, step, False).start()
 
     received[me] = outgoing[me]
-    batch = -(-(ctx_size - 1) // (z_size + 2 - ROW_FROM))
-
-    def send_batch(t):
-        @pl.when(t >= ROW_FROM)
-        def _():
-            def run(at, carry):
-                step = (t - ROW_FROM) * batch + at + 1
-
-                @pl.when(step < ctx_size)
+    turns = own_pieces * (z_size + 1)
+    batch = max(-(-(ctx_size - 1) // (turns // 2)), 1)
+
+    def send_batch(t, n):
+        if n % 2 == 0:
+            first_step = ((t - 1) * -(-own_pieces // 2) + n // 2) * batch + 1
+            for at in range(batch):
+
+                @pl.when(first_step + at < ctx_size)
                 def _():
-                    send_rows(step)
-
-                return carry
-
-            lax.fori_loop(0, batch, run, 0)
-
-    def pass_z(z_at, rising):
-        for n in range(own_pieces):
-            arrived(own_piece(n), index(z_at, y, core))
-            if rising:
-
-                @pl.when(z < z_size - 1)
-                def _():
-                    up(n, z_at).start()
-
-            else:
-
-                @pl.when(z > 0)
-                def _():
-                    down(n, z_at).start()
-
-            if y_size > 1:
-                across(n, z_at).start()
-            if n < swapped:
-                over(n, z_at, y).start()
-            beside(own_piece(n), z_at, y).start()
-
-    def pass_y(z_at):
-        for n in range(own_pieces):
-            arrived(own_piece(n), index(z_at, y_size - 1 - y, core))
-            if n < swapped:
-                over(n, z_at, y_size - 1 - y).start()
-            beside(own_piece(n), z_at, y_size - 1 - y).start()
-
-    def pass_x(z_at, y_at):
-        for n in range(swapped):
-            arrived(other_piece(n), index(z_at, y_at, core))
-            beside(other_piece(n), z_at, y_at).start()
+                    send_rows(lax.rem((first_step + at) * 7, ctx_size))
+
+    def pass_z(n, z_at, rising):
+        arrived(own_piece(n), index(z_at, y, core))
+        if rising:
+
+            @pl.when(z < z_size - 1)
+            def _():
+                up(n, z_at).start()
+
+        else:
+
+            @pl.when(z > 0)
+            def _():
+                down(n, z_at).start()
+
+        if y_size > 1:
+            across(n, z_at).start()
+        if n < swapped:
+            over(n, z_at, y).start()
+        beside(own_piece(n), z_at, y).start()
+
+    def pass_y(n, z_at):
+        arrived(own_piece(n), index(z_at, y_size - 1 - y, core))
+        if n < swapped:
+            over(n, z_at, y_size - 1 - y).start()
+        beside(own_piece(n), z_at, y_size - 1 - y).start()
+
+    def pass_x(n, z_at, y_at):
+        arrived(other_piece(n), index(z_at, y_at, core))
+        beside(other_piece(n), z_at, y_at).start()
 
     def at_distance(d, body):
         @pl.when((d >= 0) & (z - d >= 0))
@@ -316,32 +309,35 @@
         def _():
             body(z + d, False)
 
-    def forward(t, carry):
-        send_batch(t)
-        @pl.when((t > 0) & (t < z_size))
+    def forward_piece(n, t):
+        @pl.when(t < z_size)
         def _():
-            at_distance(t, pass_z)
+            at_distance(t, lambda z_at, rising: pass_z(n, z_at, rising))
 
         if y_size > 1:
 
             @pl.when(t - 1 < z_size)
             def _():
-                at_distance(t - 1, lambda z_at, rising: pass_y(z_at))
-
-        if shared:
+                at_distance(t - 1, lambda z_at, rising: pass_y(n, z_at))
+
+        if n < swapped:
 
             def both(z_at, rising):
                 @pl.when(z_at != z)
                 def _():
-                    pass_x(z_at, y)
+                    pass_x(n, z_at, y)
 
                 if y_size > 1:
-                    pass_x(z_at, y_size - 1 - y)
+                    pass_x(n, z_at, y_size - 1 - y)
 
             @pl.when(t - 2 < z_size)
             def _():
                 at_distance(t - 2, both)
 
+    def forward(t, carry):
+        for n in range(own_pieces):
+            send_batch(t, n)
+            forward_piece(n, t)
         return carry
 
     lax.fori_loop(1, z_size + 2, forward, 0)
@@ -389,7 +385,7 @@
     )
 
     each_peer(lambda step: part_copy(bias_parts, bias_send, bias_recv, step, True).wait_recv())
-    bias_ref[...] = jnp.sum(bias_parts[...], axis=0) * scale
+    bias_ref[...] = (jnp.sum(bias_parts[...], axis=0) * scale).reshape(bias_ref.shape)
 
     def sent_z(z_at, carry):
         for n in range(own_pieces):
@@ -432,7 +428,7 @@
     each_peer(
         lambda step: part_copy(hidden_parts, hidden_send, hidden_recv, step, True).wait_recv()
     )
-    hidden_ref[...] = jnp.sum(hidden_parts[...], axis=0) * scale
+    hidden_ref[...] = (jnp.sum(hidden_parts[...], axis=0) * scale).reshape(hidden_ref.shape)
     each_peer(
         lambda step: part_copy(hidden_parts, hidden_send, hidden_recv, step, False).wait_send()
     )
@@ -459,8 +455,8 @@
         ),
         out_shape=(
             jax.ShapeDtypeStruct((owned, hidden), jnp.bfloat16),
-            jax.ShapeDtypeStruct((1, hidden), jnp.float32),
-            jax.ShapeDtypeStruct((1, row_width), jnp.float32),
+            jax.ShapeDtypeStruct((hidden,), jnp.float32),
+            jax.ShapeDtypeStruct((row_width,), jnp.float32),
         ),
         in_specs=[vmem] * 3 + [pl.BlockSpec(memory_space=pl.ANY)] * 3,
         out_specs=(vmem, vmem, vmem),
@@ -502,7 +498,7 @@
         pre_act,
         proj_weight,
     )
-    return (pre_act_grad, hidden_sum.reshape(hidden), out_sum.reshape(row_width))
+    return (pre_act_grad, hidden_sum, out_sum)
 
 
 def solution(mesh):

time: 85 us -> 76.7 us (0.902)
  Pallas kernels: 80 us -> 72.4 us
  other arithmetic: 1.33 us -> 0 us
    pallas_call x1, Pallas kernels: 80 us -> 72.4 us  [per_device(): pl.pallas_call(functools.partial(kernel, grp_size, ctx_size, z_size, y_si...]
    pallas_call x1 -> x0, other arithmetic: 1.33 us -> none  [per_device(): pl.pallas_call(functools.partial(kernel, grp_size, ctx_size, z_size, y_si...]
    unnamed x4 -> x7, local copies, waits for them, and re-layouts: 2.74 us -> 3.36 us
where the time goes in v3:
time: 76.7 us; the launch traced here: 76.5 us
  Pallas kernels  72.4 us (94%)
  local copies, waits for them, and re-layouts  3.36 us (4%)
    pallas_call x1, Pallas kernels, per_device(): pl.pallas_call(functools.partial(kernel, grp_size, ctx_size, z_size, y_si...  72.4 us
    unnamed x7, local copies, waits for them, and re-layouts  3.36 us

profile of v3, /device:TPU:0, one launch (start us, length us, event | category | flops | bytes accessed | tf_op | source)
XLA Modules:
  0.0 76.5 jit_solution(12172194346439393474)
XLA Ops:
  0.6 72.4 %shard_map.85 = (bf16[192,2304]{1,0:T(8,128)(2,1)}, f32[2304]{0:T(1024)}, f32[2048]{0:T(1024)}) custom-call(s32[16]{0:T(128)} %count_ref.1, s32[384]{0:T(512)} %pos_ref.1, s32[3072]{0:T(1024)} %owner_ref.1, bf16[384,2048]{1,0:T(8,128)(2,1)} %cot_hbm.1, bf16[192,2304]{1,0:T(8,128)(2,1)} %pre_hbm.1, bf16[144,2048]{1,0:T(8,128)(2,1)} %w_hbm.1), custom_call_target="tpu_custom_call" | custom-call | flops 1811939328 | bytes 3145728 | tf_op jit(solution)/shard_map/pallas_call | solution.py:452
  73.1 0.0 copy-start
  73.1 0.0 copy-start.1
  73.1 2.1 %copy.12 = bf16[192,2304]{1,0:T(8,128)(2,1)} copy(bf16[192,2304]{1,0:T(8,128)(2,1)} %get-tuple-element.6) | data formatting | bytes 1769472
  75.3 0.0 copy-done
  75.3 0.6 copy.13
  75.9 0.0 copy-done.1
  75.9 0.6 copy.14
Async XLA Ops:
  73.1 2.2 %copy-start = (f32[2304]{0:T(1024)S(1)}, f32[2304]{0:T(1024)}, u32[]{:S(2)}) copy-start(f32[2304]{0:T(1024)} %get-tuple-element.7) | copy-start | bytes 27652
  73.1 2.8 %copy-start.1 = (f32[2048]{0:T(1024)S(1)}, f32[2048]{0:T(1024)}, u32[]{:S(2)}) copy-start(f32[2048]{0:T(1024)} %get-tuple-element.8) | copy-start | bytes 24580

commit v4 on v3

--- a/solution.py
+++ b/solution.py
@@ -259,11 +259,11 @@
 
     received[me] = outgoing[me]
     turns = own_pieces * (z_size + 1)
-    batch = max(-(-(ctx_size - 1) // (turns // 2)), 1)
+    batch = max(-(-(ctx_size - 1) // (turns // 1)), 1)
 
     def send_batch(t, n):
-        if n % 2 == 0:
-            first_step = ((t - 1) * -(-own_pieces // 2) + n // 2) * batch + 1
+        if n % 1 == 0:
+            first_step = ((t - 1) * -(-own_pieces // 1) + n // 1) * batch + 1
             for at in range(batch):
 
                 @pl.when(first_step + at < ctx_size)

time: 76.7 us -> 76.1 us (level)
  no operation moved by 1% of the time
where the time goes in v4:
time: 76.1 us; the launch traced here: 75.9 us
  Pallas kernels  71.8 us (94%)
  local copies, waits for them, and re-layouts  3.36 us (4%)
    pallas_call x1, Pallas kernels, per_device(): pl.pallas_call(functools.partial(kernel, grp_size, ctx_size, z_size, y_si...  71.8 us
    unnamed x7, local copies, waits for them, and re-layouts  3.36 us

profile of v4, /device:TPU:0, one launch (start us, length us, event | category | flops | bytes accessed | tf_op | source)
XLA Modules:
  0.0 75.9 jit_solution(17056844303404996665)
XLA Ops:
  0.6 71.8 %shard_map.85 = (bf16[192,2304]{1,0:T(8,128)(2,1)}, f32[2304]{0:T(1024)}, f32[2048]{0:T(1024)}) custom-call(s32[16]{0:T(128)} %count_ref.1, s32[384]{0:T(512)} %pos_ref.1, s32[3072]{0:T(1024)} %owner_ref.1, bf16[384,2048]{1,0:T(8,128)(2,1)} %cot_hbm.1, bf16[192,2304]{1,0:T(8,128)(2,1)} %pre_hbm.1, bf16[144,2048]{1,0:T(8,128)(2,1)} %w_hbm.1), custom_call_target="tpu_custom_call" | custom-call | flops 1811939328 | bytes 3145728 | tf_op jit(solution)/shard_map/pallas_call | solution.py:452
  72.5 0.0 copy-start
  72.5 0.0 copy-start.1
  72.5 2.1 %copy.12 = bf16[192,2304]{1,0:T(8,128)(2,1)} copy(bf16[192,2304]{1,0:T(8,128)(2,1)} %get-tuple-element.6) | data formatting | bytes 1769472
  74.7 0.0 copy-done
  74.7 0.6 copy.13
  75.3 0.0 copy-done.1
  75.3 0.6 copy.14
Async XLA Ops:
  72.5 2.2 %copy-start = (f32[2304]{0:T(1024)S(1)}, f32[2304]{0:T(1024)}, u32[]{:S(2)}) copy-start(f32[2304]{0:T(1024)} %get-tuple-element.7) | copy-start | bytes 27652
  72.5 2.8 %copy-start.1 = (f32[2048]{0:T(1024)S(1)}, f32[2048]{0:T(1024)}, u32[]{:S(2)}) copy-start(f32[2048]{0:T(1024)} %get-tuple-element.8) | copy-start | bytes 24580
